TPU v7x, 512 devices: a whole 4x4x16 slice. The times are simulated.
512 devices in a mesh: leaf: 64 (over z, y), front: 8 (over x, core).
Axes of the slice: x: 4, y: 4, z: 16, core: 2. Of those that a mesh axis runs over, the one named last changes fastest.
Arguments:
- top_factor: float32 [1408, 2816], P('front', 'leaf'), may hold values from -1 to 3
- panel_two: float32 [1408, 5632], P('front', 'leaf'), may hold values from -0.109375 to 0.109375
- panel_three: float32 [1408, 11264], P('front', 'leaf'), may hold values from -0.109375 to 0.109375
- panel_four: float32 [1408, 22528], P('front', 'leaf'), may hold values from -0.109375 to 0.109375
- factor_two: float32 [1408, 5632], P('front', 'leaf'), may hold values from -1 to 3
- factor_three: float32 [1408, 11264], P('front', 'leaf'), may hold values from -1 to 3
- factor_four: float32 [1408, 22528], P('front', 'leaf'), may hold values from -1 to 3
Outputs:
- cov_one: float32 [1408, 2816], P('front', 'leaf')
- cross_two: float32 [1408, 5632], P('front', 'leaf')
- cov_two: float32 [1408, 5632], P('front', 'leaf')
- cross_three: float32 [1408, 11264], P('front', 'leaf')
- cov_three: float32 [1408, 11264], P('front', 'leaf')
- cross_four: float32 [1408, 22528], P('front', 'leaf')
- cov_four: float32 [1408, 22528], P('front', 'leaf')
All inputs are finite; a program needn't handle non-finite values.
Results may differ from a plain program's by a relative error of at most 0.000088.
Values sent between devices are 32-bit elements; how exact they have to be, the bound alone decides.
No kernel may reach another device: no remote copies, remote signals or barrier semaphores. Data moves between devices by JAX's collectives and lax.ppermute only.
A program may use at most 64 MiB of HBM per device.

v0:
```python
import jax
import jax.numpy as jnp
from jax import lax
from jax.sharding import PartitionSpec as P

S = 1408


def from_partner(value, axis, distance):
    mask = 2**distance
    pairs = [(source, source ^ mask) for source in range(lax.axis_size(axis))]
    return lax.ppermute(value, axis, pairs)


def product(first, second):
    return jnp.dot(
        first, second, precision=lax.Precision.HIGHEST, preferred_element_type=jnp.float32
    )


def inner_product(first, second):
    return lax.dot_general(
        first,
        second,
        (((0,), (0,)), ((), ())),
        precision=lax.Precision.HIGHEST,
        preferred_element_type=jnp.float32,
    )


def cube_rows(block_tile, cube_size):
    position = lax.axis_index("leaf")
    joined = block_tile
    for bit_index in range(cube_size.bit_length() - 1):
        partner = from_partner(joined, "leaf", bit_index)
        is_upper = jnp.right_shift(position, bit_index) % 2 == 1
        joined = jnp.where(
            is_upper, jnp.concatenate([partner, joined], -1), jnp.concatenate([joined, partner], -1)
        )
    return joined


def local(top_factor, panel_two, panel_three, panel_four, factor_two, factor_three, factor_four):
    share_rows = S // lax.axis_size("front")

    def front_sum(term_fn):
        return lax.psum_scatter(
            term_fn(jnp.int32(0), share_rows * lax.axis_size("front")),
            "front",
            scatter_dimension=0,
            tiled=True,
        )

    top_rows = cube_rows(top_factor, S // top_factor.shape[1])

    def top_term(offset, amount):
        return inner_product(top_rows, top_factor)

    parent = front_sum(top_term)
    results = [parent]
    for panel_tile, factor_tile in (
        (panel_two, factor_two),
        (panel_three, factor_three),
        (panel_four, factor_four),
    ):
        tile_width = panel_tile.shape[1]
        cube_size = S // tile_width
        parent_rows = cube_rows(parent, S // parent.shape[1])
        cross_block = -product(parent_rows, lax.all_gather(panel_tile, "front", axis=0, tiled=True))
        stacked = cube_rows(jnp.stack([cross_block, factor_tile]), cube_size)

        def level_term(offset, amount):
            gram_part = inner_product(stacked[1], factor_tile)
            return gram_part - inner_product(stacked[0], panel_tile)

        covariance = front_sum(level_term)
        results.append(cross_block)
        results.append(covariance)
        parent = covariance
    return tuple(results)


def solution(mesh):
    return jax.shard_map(
        local,
        mesh=mesh,
        in_specs=(
            P("front", "leaf"),
            P("front", "leaf"),
            P("front", "leaf"),
            P("front", "leaf"),
            P("front", "leaf"),
            P("front", "leaf"),
            P("front", "leaf"),
        ),
        out_specs=(
            P("front", "leaf"),
            P("front", "leaf"),
            P("front", "leaf"),
            P("front", "leaf"),
            P("front", "leaf"),
            P("front", "leaf"),
            P("front", "leaf"),
        ),
        check_vma=False,
    )
```

profile of v0, /device:TPU:8, one launch (start us, length us, event | category | flops | bytes accessed | tf_op | source)
XLA Modules:
  0.0 660.0 jit_solution(10126110818156442605)
XLA Ops:
  8.1 7.7 %collective-permute-start = (f32[176,44]{1,0:T(8,128)S(1)}, f32[176,44]{1,0:T(8,128)S(1)}, u32[]{:S(2)}, u32[]{:S(2)}) collective-permute-start(f32[176,44]{1,0:T(8,128)S(1)} %copy.16), channel_id=1, source_target_pairs={{0,8},{8,0},{16,24},{24,16},{32,40},{40,32},{48,56},{56,48},{64,72... | collective-permute-start | bytes 92936 | tf_op jit(solution)/shard_map/ppermute | solution.py:12
  28.5 6.7 %collective-permute-done.2 = f32[176,176]{1,0:T(8,128)S(1)} collective-permute-done((f32[176,176]{1,0:T(8,128)S(1)}, f32[176,176]{1,0:T(8,128)S(1)}, u32[]{:S(2)}, u32[]{:S(2)}) %collective-permute-start.2) | collective-permute-done | bytes 123936 | tf_op jit(solution)/shard_map/ppermute | solution.py:12
  37.3 9.2 %collective-permute-done.3 = f32[176,352]{1,0:T(8,128)S(1)} collective-permute-done((f32[176,352]{1,0:T(8,128)S(1)}, f32[176,352]{1,0:T(8,128)S(1)}, u32[]{:S(2)}, u32[]{:S(2)}) %collective-permute-start.3) | collective-permute-done | bytes 247840 | tf_op jit(solution)/shard_map/ppermute | solution.py:12
  46.8 7.1 %collective-permute-start.4 = (f32[176,704]{1,0:T(8,128)S(1)}, f32[176,704]{1,0:T(8,128)S(1)}, u32[]{:S(2)}, u32[]{:S(2)}) collective-permute-start(f32[176,704]{1,0:T(8,128)S(1)} %maximum_select_fusion.15), channel_id=1, source_target_pairs={{0,128},{8,136},{16,144},{24,152},{32,160},{40,168},{48,176},{56,1... | collective-permute-start | bytes 1486856 | tf_op jit(solution)/shard_map/ppermute | solution.py:12
  53.9 44.9 %collective-permute-done.4 = f32[176,704]{1,0:T(8,128)S(1)} collective-permute-done((f32[176,704]{1,0:T(8,128)S(1)}, f32[176,704]{1,0:T(8,128)S(1)}, u32[]{:S(2)}, u32[]{:S(2)}) %collective-permute-start.4) | collective-permute-done | bytes 495648 | tf_op jit(solution)/shard_map/ppermute | solution.py:12
  102.5 40.2 %reduce-scatter.13.cloned.1.call-done = f32[176,44]{1,0:T(8,128)} async-done(((f32[1408,44]{1,0:T(8,128)}), f32[176,44]{1,0:T(8,128)}) %reduce-scatter.13.cloned.1.call-update) | async-done | bytes 30992 | tf_op jit(solution)/shard_map/reduce_scatter | solution.py:47
  172.2 7.6 %collective-permute-done.8 = f32[176,352]{1,0:T(8,128)S(1)} collective-permute-done((f32[176,352]{1,0:T(8,128)S(1)}, f32[176,352]{1,0:T(8,128)S(1)}, u32[]{:S(2)}, u32[]{:S(2)}) %collective-permute-start.8) | collective-permute-done | bytes 247840 | tf_op jit(solution)/shard_map/ppermute | solution.py:12
  180.0 22.2 %collective-permute-start.9 = (f32[176,704]{1,0:T(8,128)S(1)}, f32[176,704]{1,0:T(8,128)S(1)}, u32[]{:S(2)}, u32[]{:S(2)}) collective-permute-start(f32[176,704]{1,0:T(8,128)S(1)} %maximum_select_fusion.16), channel_id=1, source_target_pairs={{0,128},{8,136},{16,144},{24,152},{32,160},{40,168},{48,176},{56,1... | collective-permute-start | bytes 1486856 | tf_op jit(solution)/shard_map/ppermute | solution.py:12
  202.4 13.3 %all_gather.9 = f32[1408,88]{1,0:T(8,128)S(1)} all-gather(f32[176,88]{1,0:T(8,128)S(1)} %copy-done.6), channel_id=1, replica_groups=mesh['leaf'=64,'front'=8] {'front'}, dimensions={0}, use_global_device_ids=true | all-gather | bytes 557568 | tf_op jit(solution)/shard_map/all_gather | solution.py:69
  215.7 10.3 %collective-permute-done.9 = f32[176,704]{1,0:T(8,128)S(1)} collective-permute-done((f32[176,704]{1,0:T(8,128)S(1)}, f32[176,704]{1,0:T(8,128)S(1)}, u32[]{:S(2)}, u32[]{:S(2)}) %collective-permute-start.9) | collective-permute-done | bytes 495648 | tf_op jit(solution)/shard_map/ppermute | solution.py:12
  239.2 6.8 %collective-permute-done.11 = f32[2,176,176]{1,2,0:T(8,128)S(1)} collective-permute-done((f32[2,176,176]{1,2,0:T(8,128)S(1)}, f32[2,176,176]{1,2,0:T(8,128)S(1)}, u32[]{:S(2)}, u32[]{:S(2)}) %collective-permute-start.11) | collective-permute-done | bytes 247840 | tf_op jit(solution)/shard_map/ppermute | solution.py:12
  248.2 9.3 %collective-permute-done.12 = f32[2,176,352]{2,1,0:T(8,128)S(1)} collective-permute-done((f32[2,176,352]{2,1,0:T(8,128)S(1)}, f32[2,176,352]{2,1,0:T(8,128)S(1)}, u32[]{:S(2)}, u32[]{:S(2)}) %collective-permute-start.12) | collective-permute-done | bytes 495648 | tf_op jit(solution)/shard_map/ppermute | solution.py:12
  258.4 8.6 %collective-permute-start.13 = (f32[2,176,704]{2,1,0:T(8,128)S(1)}, f32[2,176,704]{2,1,0:T(8,128)}, u32[]{:S(2)}, u32[]{:S(2)}) collective-permute-start(f32[2,176,704]{2,1,0:T(8,128)S(1)} %copy.26), channel_id=1, source_target_pairs={{0,64},{8,72},{16,80},{24,88},{32,96},{40,104},{48,112},{56,120},{... | collective-permute-start | bytes 2973704 | tf_op jit(solution)/shard_map/ppermute | solution.py:12
  267.0 44.9 %collective-permute-done.13 = f32[2,176,704]{2,1,0:T(8,128)} collective-permute-done((f32[2,176,704]{2,1,0:T(8,128)S(1)}, f32[2,176,704]{2,1,0:T(8,128)}, u32[]{:S(2)}, u32[]{:S(2)}) %collective-permute-start.13) | collective-permute-done | bytes 991264 | tf_op jit(solution)/shard_map/ppermute | solution.py:12
  317.5 47.1 %reduce-scatter.7.cloned.1.call-done = f32[176,88]{1,0:T(8,128)} async-done(((f32[1408,88]{1,0:T(8,128)}), f32[176,88]{1,0:T(8,128)}) %reduce-scatter.7.cloned.1.call-update) | async-done | bytes 61968 | tf_op jit(solution)/shard_map/reduce_scatter | solution.py:47
  396.0 14.6 %all_gather.10 = f32[1408,176]{1,0:T(8,128)S(1)} all-gather(f32[176,176]{1,0:T(8,128)S(1)} %copy-done.5), channel_id=1, replica_groups=mesh['leaf'=64,'front'=8] {'front'}, dimensions={0}, use_global_device_ids=true | all-gather | bytes 1115136 | tf_op jit(solution)/shard_map/all_gather | solution.py:69
  417.1 7.4 %collective-permute-done.18 = f32[2,176,176]{2,1,0:T(8,128)S(1)} collective-permute-done((f32[2,176,176]{2,1,0:T(8,128)S(1)}, f32[2,176,176]{2,1,0:T(8,128)S(1)}, u32[]{:S(2)}, u32[]{:S(2)}) %collective-permute-start.18) | collective-permute-done | bytes 247840 | tf_op jit(solution)/shard_map/ppermute | solution.py:12
  428.8 11.1 %collective-permute-done.19 = f32[2,176,352]{2,1,0:T(8,128)S(1)} collective-permute-done((f32[2,176,352]{2,1,0:T(8,128)S(1)}, f32[2,176,352]{2,1,0:T(8,128)S(1)}, u32[]{:S(2)}, u32[]{:S(2)}) %collective-permute-start.19) | collective-permute-done | bytes 495648 | tf_op jit(solution)/shard_map/ppermute | solution.py:12
  442.6 22.2 %collective-permute-done.20 = f32[2,176,704]{2,1,0:T(8,128)S(1)} collective-permute-done((f32[2,176,704]{2,1,0:T(8,128)S(1)}, f32[2,176,704]{2,1,0:T(8,128)S(1)}, u32[]{:S(2)}, u32[]{:S(2)}) %collective-permute-start.20) | collective-permute-done | bytes 991264 | tf_op jit(solution)/shard_map/ppermute | solution.py:12
  472.0 49.3 %reduce-scatter.9.cloned.1.call-done = f32[176,176]{1,0:T(8,128)} async-done(((f32[1408,176]{1,0:T(8,128)}), f32[176,176]{1,0:T(8,128)}) %reduce-scatter.9.cloned.1.call-update) | async-done | bytes 123920 | tf_op jit(solution)/shard_map/reduce_scatter | solution.py:47
  543.9 11.3 %all-gather.2.cloned.1.call-done = f32[1408,352]{1,0:T(8,128)} async-done(((f32[176,352]{1,0:T(8,128)}), f32[1408,352]{1,0:T(8,128)}) %all-gather.2.cloned.1.call-update) | async-done | bytes 1982480 | tf_op jit(solution)/shard_map/all_gather | solution.py:69
  561.7 13.6 %collective-permute-done.24 = f32[2,176,352]{2,1,0:T(8,128)S(1)} collective-permute-done((f32[2,176,352]{2,1,0:T(8,128)S(1)}, f32[2,176,352]{2,1,0:T(8,128)S(1)}, u32[]{:S(2)}, u32[]{:S(2)}) %collective-permute-start.24) | collective-permute-done | bytes 495648 | tf_op jit(solution)/shard_map/ppermute | solution.py:12
  579.9 24.6 %collective-permute-done.25 = f32[2,176,704]{2,1,0:T(8,128)S(1)} collective-permute-done((f32[2,176,704]{2,1,0:T(8,128)S(1)}, f32[2,176,704]{2,1,0:T(8,128)S(1)}, u32[]{:S(2)}, u32[]{:S(2)}) %collective-permute-start.25) | collective-permute-done | bytes 991264 | tf_op jit(solution)/shard_map/ppermute | solution.py:12
  614.0 39.5 %reduce-scatter.11.cloned.1.call-done = f32[176,352]{1,0:T(8,128)} async-done(((f32[1408,352]{1,0:T(8,128)}), f32[176,352]{1,0:T(8,128)}) %reduce-scatter.11.cloned.1.call-update) | async-done | bytes 247824 | tf_op jit(solution)/shard_map/reduce_scatter | solution.py:47
  (108 shorter events, 166.1 us)
Async XLA Ops:
  7.2 135.6 %reduce-scatter.13.cloned.1.call-start = ((), (), s32[]{:S(2)}) async-start(), calls=%async_computation.8 | async-start | bytes 811008 | tf_op jit(solution)/shard_map/reduce_scatter | solution.py:47
  8.1 10.2 %collective-permute-start = (f32[176,44]{1,0:T(8,128)S(1)}, f32[176,44]{1,0:T(8,128)S(1)}, u32[]{:S(2)}, u32[]{:S(2)}) collective-permute-start(f32[176,44]{1,0:T(8,128)S(1)} %copy.16), channel_id=1, source_target_pairs={{0,8},{8,0},{16,24},{24,16},{32,40},{40,32},{48,56},{56,48},{64,72... | collective-permute-start | bytes 92936 | tf_op jit(solution)/shard_map/ppermute | solution.py:12
  35.4 11.1 %collective-permute-start.3 = (f32[176,352]{1,0:T(8,128)S(1)}, f32[176,352]{1,0:T(8,128)S(1)}, u32[]{:S(2)}, u32[]{:S(2)}) collective-permute-start(f32[176,352]{1,0:T(8,128)S(1)} %maximum_select_fusion.21), channel_id=1, source_target_pairs={{0,64},{8,72},{16,80},{24,88},{32,96},{40,104},{48,112},{56,120},{... | collective-permute-start | bytes 743432 | tf_op jit(solution)/shard_map/ppermute | solution.py:12
  46.8 52.1 %collective-permute-start.4 = (f32[176,704]{1,0:T(8,128)S(1)}, f32[176,704]{1,0:T(8,128)S(1)}, u32[]{:S(2)}, u32[]{:S(2)}) collective-permute-start(f32[176,704]{1,0:T(8,128)S(1)} %maximum_select_fusion.15), channel_id=1, source_target_pairs={{0,128},{8,136},{16,144},{24,152},{32,160},{40,168},{48,176},{56,1... | collective-permute-start | bytes 1486856 | tf_op jit(solution)/shard_map/ppermute | solution.py:12
  102.5 262.1 %reduce-scatter.7.cloned.1.call-start = ((), (), s32[]{:S(2)}) async-start(), calls=%async_computation.4 | async-start | bytes 811008 | tf_op jit(solution)/shard_map/reduce_scatter | solution.py:47
  158.6 9.0 %collective-permute-start.7 = (f32[176,176]{1,0:T(8,128)S(1)}, f32[176,176]{1,0:T(8,128)S(1)}, u32[]{:S(2)}, u32[]{:S(2)}) collective-permute-start(f32[176,176]{1,0:T(8,128)S(1)} %maximum_select_fusion.26), channel_id=1, source_target_pairs={{0,32},{8,40},{16,48},{24,56},{32,0},{40,8},{48,16},{56,24},{64,96... | collective-permute-start | bytes 371720 | tf_op jit(solution)/shard_map/ppermute | solution.py:12
  167.7 12.1 %collective-permute-start.8 = (f32[176,352]{1,0:T(8,128)S(1)}, f32[176,352]{1,0:T(8,128)S(1)}, u32[]{:S(2)}, u32[]{:S(2)}) collective-permute-start(f32[176,352]{1,0:T(8,128)S(1)} %maximum_select_fusion.22), channel_id=1, source_target_pairs={{0,64},{8,72},{16,80},{24,88},{32,96},{40,104},{48,112},{56,120},{... | collective-permute-start | bytes 743432 | tf_op jit(solution)/shard_map/ppermute | solution.py:12
  180.0 45.9 %collective-permute-start.9 = (f32[176,704]{1,0:T(8,128)S(1)}, f32[176,704]{1,0:T(8,128)S(1)}, u32[]{:S(2)}, u32[]{:S(2)}) collective-permute-start(f32[176,704]{1,0:T(8,128)S(1)} %maximum_select_fusion.16), channel_id=1, source_target_pairs={{0,128},{8,136},{16,144},{24,152},{32,160},{40,168},{48,176},{56,1... | collective-permute-start | bytes 1486856 | tf_op jit(solution)/shard_map/ppermute | solution.py:12
  235.1 10.8 %collective-permute-start.11 = (f32[2,176,176]{1,2,0:T(8,128)S(1)}, f32[2,176,176]{1,2,0:T(8,128)S(1)}, u32[]{:S(2)}, u32[]{:S(2)}) collective-permute-start(f32[2,176,176]{1,2,0:T(8,128)S(1)} %maximum_select_fusion.20), channel_id=1, source_target_pairs={{0,16},{8,24},{16,0},{24,8},{32,48},{40,56},{48,32},{56,40},{64,80... | collective-permute-start | bytes 743432 | tf_op jit(solution)/shard_map/ppermute | solution.py:12
  246.3 11.3 %collective-permute-start.12 = (f32[2,176,352]{2,1,0:T(8,128)S(1)}, f32[2,176,352]{2,1,0:T(8,128)S(1)}, u32[]{:S(2)}, u32[]{:S(2)}) collective-permute-start(f32[2,176,352]{2,1,0:T(8,128)S(1)} %copy.23), channel_id=1, source_target_pairs={{0,32},{8,40},{16,48},{24,56},{32,0},{40,8},{48,16},{56,24},{64,96... | collective-permute-start | bytes 1486856 | tf_op jit(solution)/shard_map/ppermute | solution.py:12
  258.4 53.5 %collective-permute-start.13 = (f32[2,176,704]{2,1,0:T(8,128)S(1)}, f32[2,176,704]{2,1,0:T(8,128)}, u32[]{:S(2)}, u32[]{:S(2)}) collective-permute-start(f32[2,176,704]{2,1,0:T(8,128)S(1)} %copy.26), channel_id=1, source_target_pairs={{0,64},{8,72},{16,80},{24,88},{32,96},{40,104},{48,112},{56,120},{... | collective-permute-start | bytes 2973704 | tf_op jit(solution)/shard_map/ppermute | solution.py:12
  317.4 203.9 %reduce-scatter.9.cloned.1.call-start = ((), (), s32[]{:S(2)}) async-start(), calls=%async_computation.5 | async-start | bytes 1622016 | tf_op jit(solution)/shard_map/reduce_scatter | solution.py:47
  372.3 8.9 %collective-permute-start.15 = (f32[176,176]{1,0:T(8,128)S(1)}, f32[176,176]{1,0:T(8,128)S(1)}, u32[]{:S(2)}, u32[]{:S(2)}) collective-permute-start(f32[176,176]{1,0:T(8,128)S(1)} %maximum_select_fusion.27), channel_id=1, source_target_pairs={{0,16},{8,24},{16,0},{24,8},{32,48},{40,56},{48,32},{56,40},{64,80... | collective-permute-start | bytes 371720 | tf_op jit(solution)/shard_map/ppermute | solution.py:12
  381.4 9.9 %collective-permute-start.16 = (f32[176,352]{1,0:T(8,128)S(1)}, f32[176,352]{1,0:T(8,128)S(1)}, u32[]{:S(2)}, u32[]{:S(2)}) collective-permute-start(f32[176,352]{1,0:T(8,128)S(1)} %maximum_select_fusion.23), channel_id=1, source_target_pairs={{0,32},{8,40},{16,48},{24,56},{32,0},{40,8},{48,16},{56,24},{64,96... | collective-permute-start | bytes 743432 | tf_op jit(solution)/shard_map/ppermute | solution.py:12
  391.6 20.8 %collective-permute-start.17 = (f32[176,704]{1,0:T(8,128)S(1)}, f32[176,704]{1,0:T(8,128)S(1)}, u32[]{:S(2)}, u32[]{:S(2)}) collective-permute-start(f32[176,704]{1,0:T(8,128)S(1)} %maximum_select_fusion.17), channel_id=1, source_target_pairs={{0,64},{8,72},{16,80},{24,88},{32,96},{40,104},{48,112},{56,120},{... | collective-permute-start | bytes 1486856 | tf_op jit(solution)/shard_map/ppermute | solution.py:12
  413.7 10.8 %collective-permute-start.18 = (f32[2,176,176]{2,1,0:T(8,128)S(1)}, f32[2,176,176]{2,1,0:T(8,128)S(1)}, u32[]{:S(2)}, u32[]{:S(2)}) collective-permute-start(f32[2,176,176]{2,1,0:T(8,128)S(1)} %pad_maximum_fusion.1), channel_id=1, source_target_pairs={{0,8},{8,0},{16,24},{24,16},{32,40},{40,32},{48,56},{56,48},{64,72... | collective-permute-start | bytes 743432 | tf_op jit(solution)/shard_map/ppermute | solution.py:12
  424.7 15.2 %collective-permute-start.19 = (f32[2,176,352]{2,1,0:T(8,128)S(1)}, f32[2,176,352]{2,1,0:T(8,128)S(1)}, u32[]{:S(2)}, u32[]{:S(2)}) collective-permute-start(f32[2,176,352]{2,1,0:T(8,128)S(1)} %maximum_select_fusion.18), channel_id=1, source_target_pairs={{0,16},{8,24},{16,0},{24,8},{32,48},{40,56},{48,32},{56,40},{64,80... | collective-permute-start | bytes 1486856 | tf_op jit(solution)/shard_map/ppermute | solution.py:12
  440.4 24.4 %collective-permute-start.20 = (f32[2,176,704]{2,1,0:T(8,128)S(1)}, f32[2,176,704]{2,1,0:T(8,128)S(1)}, u32[]{:S(2)}, u32[]{:S(2)}) collective-permute-start(f32[2,176,704]{2,1,0:T(8,128)S(1)} %maximum_select_fusion.4), channel_id=1, source_target_pairs={{0,32},{8,40},{16,48},{24,56},{32,0},{40,8},{48,16},{56,24},{64,96... | collective-permute-start | bytes 2973704 | tf_op jit(solution)/shard_map/ppermute | solution.py:12
  471.4 83.8 %all-gather.2.cloned.1.call-start = ((), (), s32[]{:S(2)}) async-start(), calls=%async_computation.6 | async-start | bytes 2433024 | tf_op jit(solution)/shard_map/all_gather | solution.py:69
  472.0 181.5 %reduce-scatter.11.cloned.1.call-start = ((), (), s32[]{:S(2)}) async-start(), calls=%async_computation.7 | async-start | bytes 2433024 | tf_op jit(solution)/shard_map/reduce_scatter | solution.py:47
  530.1 9.9 %collective-permute-start.22 = (f32[176,352]{1,0:T(8,128)S(1)}, f32[176,352]{1,0:T(8,128)S(1)}, u32[]{:S(2)}, u32[]{:S(2)}) collective-permute-start(f32[176,352]{1,0:T(8,128)S(1)} %maximum_select_fusion.24), channel_id=1, source_target_pairs={{0,16},{8,24},{16,0},{24,8},{32,48},{40,56},{48,32},{56,40},{64,80... | collective-permute-start | bytes 743432 | tf_op jit(solution)/shard_map/ppermute | solution.py:12
  540.3 15.0 %collective-permute-start.23 = (f32[176,704]{1,0:T(8,128)S(1)}, f32[176,704]{1,0:T(8,128)S(1)}, u32[]{:S(2)}, u32[]{:S(2)}) collective-permute-start(f32[176,704]{1,0:T(8,128)S(1)} %maximum_select_fusion.19), channel_id=1, source_target_pairs={{0,32},{8,40},{16,48},{24,56},{32,0},{40,8},{48,16},{56,24},{64,96... | collective-permute-start | bytes 1486856 | tf_op jit(solution)/shard_map/ppermute | solution.py:12
  559.0 16.3 %collective-permute-start.24 = (f32[2,176,352]{2,1,0:T(8,128)S(1)}, f32[2,176,352]{2,1,0:T(8,128)S(1)}, u32[]{:S(2)}, u32[]{:S(2)}) collective-permute-start(f32[2,176,352]{2,1,0:T(8,128)S(1)} %pad_maximum_fusion), channel_id=1, source_target_pairs={{0,8},{8,0},{16,24},{24,16},{32,40},{40,32},{48,56},{56,48},{64,72... | collective-permute-start | bytes 1486856 | tf_op jit(solution)/shard_map/ppermute | solution.py:12
  575.8 28.6 %collective-permute-start.25 = (f32[2,176,704]{2,1,0:T(8,128)S(1)}, f32[2,176,704]{2,1,0:T(8,128)S(1)}, u32[]{:S(2)}, u32[]{:S(2)}) collective-permute-start(f32[2,176,704]{2,1,0:T(8,128)S(1)} %maximum_select_fusion.5), channel_id=1, source_target_pairs={{0,16},{8,24},{16,0},{24,8},{32,48},{40,56},{48,32},{56,40},{64,80... | collective-permute-start | bytes 2973704 | tf_op jit(solution)/shard_map/ppermute | solution.py:12
  (17 other events, 491.5 us)
Sparse Core Ops, SparseCore 0:
  102.6 40.1 reduce-scatter.12
  317.6 46.9 reduce-scatter.6
  471.5 49.7 reduce-scatter.8
  523.3 31.8 all-gather.1
  611.8 41.6 reduce-scatter.10
where the time goes:
time: 661 us; the launch traced here: 660 us
  waiting for transfers between devices  461 us (70%)
  starting transfers between devices  115 us (17%)
  blocking collectives  27.9 us (4%)
  matrix products  26.2 us (4%)
  between operations  14.4 us (2%)
  other arithmetic  8.58 us (1%)
    ppermute x26, waiting for transfers between devices, from_partner(): return lax.ppermute(value, axis, pairs)  274 us
    reduce_scatter x4, waiting for transfers between devices, front_sum(): lax.psum_scatter(term_fn(jnp.int32(0), share_rows * lax.axis_size('front'...  176 us
    ppermute x26, starting transfers between devices, from_partner(): return lax.ppermute(value, axis, pairs)  115 us
    all_gather x2, blocking collectives, local(): lax.all_gather(panel_tile, 'front', axis=0, tiled=True)  27.9 us
    dot_general x6, matrix products, inner_product(): lax.dot_general(first, second, (((0,), (0,)), ((), ())), precision=lax.Pr...  15.9 us
  transfers between devices with their start and end apart: 31, of which 30 were waited for; matrix products, arithmetic and copies ran while one was open for 0% of the time, Pallas kernels for 0%

commit v1 on v0

--- a/solution.py
+++ b/solution.py
@@ -4,6 +4,19 @@
 from jax.sharding import PartitionSpec as P
 
 S = 1408
+
+
+def collect(shard, axis, dim):
+    ways = lax.axis_size(axis)
+    up = [(d, (d + 1) % ways) for d in range(ways)]
+    down = [(d, (d - 1) % ways) for d in range(ways)]
+    earlier, later = ([shard], [shard])
+    for _ in range(ways // 2):
+        earlier.append(lax.ppermute(earlier[-1], axis, up))
+    for _ in range((ways - 1) // 2):
+        later.append(lax.ppermute(later[-1], axis, down))
+    line = jnp.concatenate([*earlier[::-1], *later[1:]], axis=dim)
+    return jnp.roll(line, (lax.axis_index(axis) - ways // 2) * shard.shape[dim], axis=dim)
 
 
 def from_partner(value, axis, distance):
@@ -66,7 +79,7 @@
         tile_width = panel_tile.shape[1]
         cube_size = S // tile_width
         parent_rows = cube_rows(parent, S // parent.shape[1])
-        cross_block = -product(parent_rows, lax.all_gather(panel_tile, "front", axis=0, tiled=True))
+        cross_block = -product(parent_rows, collect(panel_tile, "front", 0))
         stacked = cube_rows(jnp.stack([cross_block, factor_tile]), cube_size)
 
         def level_term(offset, amount):

time: 661 us -> 661 us (level)
  starting transfers between devices: 115 us -> 150 us
  blocking collectives: 27.9 us -> 0 us
  waiting for transfers between devices: 461 us -> 437 us
  local copies, waits for them, and re-layouts: 5.99 us -> 23.2 us
    reduce_scatter x4, waiting for transfers between devices: 176 us -> 119 us  [front_sum(): lax.psum_scatter(term_fn(jnp.int32(0), share_rows * lax.axis_size('front'...]
    ppermute x0 -> x21, waiting for transfers between devices: none -> 45.7 us  [the longest x12 45.7 us: collect(): earlier.append(lax.ppermute(earlier[-1], axis, up))]
    ppermute x0 -> x21, starting transfers between devices: none -> 35.7 us  [the longest x9 35.6 us: collect(): later.append(lax.ppermute(later[-1], axis, down))]
    all_gather x2 -> x0, blocking collectives: 27.9 us -> none  [local(): lax.all_gather(panel_tile, 'front', axis=0, tiled=True)]
    unnamed x24 -> x85, local copies, waits for them, and re-layouts: 3.36 us -> 18.9 us
    all_gather x1 -> x0, waiting for transfers between devices: 11.3 us -> none  [local(): lax.all_gather(panel_tile, 'front', axis=0, tiled=True)]
  transfers between devices with their start and end apart: 31 -> 51, of which waited for: 30 -> 40; matrix products, arithmetic and copies ran while one was open for 0% -> 5% of each run, Pallas kernels for 0% -> 0%
where the time goes in v1:
time: 661 us; the launch traced here: 660 us
  waiting for transfers between devices  437 us (66%)
  starting transfers between devices  150 us (23%)
  matrix products  26.7 us (4%)
  local copies, waits for them, and re-layouts  23.2 us (4%)
  between operations  14.8 us (2%)
  other arithmetic  8.54 us (1%)
    ppermute x26, waiting for transfers between devices, from_partner(): return lax.ppermute(value, axis, pairs)  272 us
    reduce_scatter x4, waiting for transfers between devices, front_sum(): lax.psum_scatter(term_fn(jnp.int32(0), share_rows * lax.axis_size('front'...  119 us
    ppermute x26, starting transfers between devices, from_partner(): return lax.ppermute(value, axis, pairs)  114 us
    ppermute x12, waiting for transfers between devices, collect(): earlier.append(lax.ppermute(earlier[-1], axis, up))  45.7 us
    ppermute x9, starting transfers between devices, collect(): later.append(lax.ppermute(later[-1], axis, down))  35.6 us
    unnamed x85, local copies, waits for them, and re-layouts  18.9 us
    dot_general x6, matrix products, inner_product(): lax.dot_general(first, second, (((0,), (0,)), ((), ())), precision=lax.Pr...  16.2 us
  transfers between devices with their start and end apart: 51, of which 40 were waited for; matrix products, arithmetic and copies ran while one was open for 5% of the time, Pallas kernels for 0%

profile of v1, /device:TPU:8, one launch (start us, length us, event | category | flops | bytes accessed | tf_op | source)
XLA Modules:
  0.0 660.1 jit_solution(686576142577961919)
XLA Ops:
  8.1 7.7 %collective-permute-start = (f32[176,44]{1,0:T(8,128)S(1)}, f32[176,44]{1,0:T(8,128)S(1)}, u32[]{:S(2)}, u32[]{:S(2)}) collective-permute-start(f32[176,44]{1,0:T(8,128)S(1)} %copy.16), channel_id=1, source_target_pairs={{0,8},{8,0},{16,24},{24,16},{32,40},{40,32},{48,56},{56,48},{64,72... | collective-permute-start | bytes 92936 | tf_op jit(solution)/shard_map/ppermute | solution.py:25
  28.5 6.7 %collective-permute-done.2 = f32[176,176]{1,0:T(8,128)S(1)} collective-permute-done((f32[176,176]{1,0:T(8,128)S(1)}, f32[176,176]{1,0:T(8,128)S(1)}, u32[]{:S(2)}, u32[]{:S(2)}) %collective-permute-start.2) | collective-permute-done | bytes 123936 | tf_op jit(solution)/shard_map/ppermute | solution.py:25
  37.5 9.2 %collective-permute-done.3 = f32[176,352]{1,0:T(8,128)S(1)} collective-permute-done((f32[176,352]{1,0:T(8,128)S(1)}, f32[176,352]{1,0:T(8,128)S(1)}, u32[]{:S(2)}, u32[]{:S(2)}) %collective-permute-start.3) | collective-permute-done | bytes 247840 | tf_op jit(solution)/shard_map/ppermute | solution.py:25
  46.9 7.1 %collective-permute-start.4 = (f32[176,704]{1,0:T(8,128)S(1)}, f32[176,704]{1,0:T(8,128)S(1)}, u32[]{:S(2)}, u32[]{:S(2)}) collective-permute-start(f32[176,704]{1,0:T(8,128)S(1)} %maximum_select_fusion.15), channel_id=1, source_target_pairs={{0,128},{8,136},{16,144},{24,152},{32,160},{40,168},{48,176},{56,1... | collective-permute-start | bytes 1486856 | tf_op jit(solution)/shard_map/ppermute | solution.py:25
  69.6 29.4 %collective-permute-done.4 = f32[176,704]{1,0:T(8,128)S(1)} collective-permute-done((f32[176,704]{1,0:T(8,128)S(1)}, f32[176,704]{1,0:T(8,128)S(1)}, u32[]{:S(2)}, u32[]{:S(2)}) %collective-permute-start.4) | collective-permute-done | bytes 495648 | tf_op jit(solution)/shard_map/ppermute | solution.py:25
  105.3 37.6 %reduce-scatter.13.cloned.1.call-done = f32[176,44]{1,0:T(8,128)} async-done(((f32[1408,44]{1,0:T(8,128)}), f32[176,44]{1,0:T(8,128)}) %reduce-scatter.13.cloned.1.call-update) | async-done | bytes 30992 | tf_op jit(solution)/shard_map/reduce_scatter | solution.py:60
  172.4 7.6 %collective-permute-done.8 = f32[176,352]{1,0:T(8,128)S(1)} collective-permute-done((f32[176,352]{1,0:T(8,128)S(1)}, f32[176,352]{1,0:T(8,128)S(1)}, u32[]{:S(2)}, u32[]{:S(2)}) %collective-permute-start.8) | collective-permute-done | bytes 247840 | tf_op jit(solution)/shard_map/ppermute | solution.py:25
  180.2 22.2 %collective-permute-start.9 = (f32[176,704]{1,0:T(8,128)S(1)}, f32[176,704]{1,0:T(8,128)S(1)}, u32[]{:S(2)}, u32[]{:S(2)}) collective-permute-start(f32[176,704]{1,0:T(8,128)S(1)} %maximum_select_fusion.16), channel_id=1, source_target_pairs={{0,128},{8,136},{16,144},{24,152},{32,160},{40,168},{48,176},{56,1... | collective-permute-start | bytes 1486856 | tf_op jit(solution)/shard_map/ppermute | solution.py:25
  202.6 23.6 %collective-permute-done.9 = f32[176,704]{1,0:T(8,128)S(1)} collective-permute-done((f32[176,704]{1,0:T(8,128)S(1)}, f32[176,704]{1,0:T(8,128)S(1)}, u32[]{:S(2)}, u32[]{:S(2)}) %collective-permute-start.9) | collective-permute-done | bytes 495648 | tf_op jit(solution)/shard_map/ppermute | solution.py:25
  239.4 6.8 %collective-permute-done.18 = f32[2,176,176]{1,2,0:T(8,128)S(1)} collective-permute-done((f32[2,176,176]{1,2,0:T(8,128)S(1)}, f32[2,176,176]{1,2,0:T(8,128)S(1)}, u32[]{:S(2)}, u32[]{:S(2)}) %collective-permute-start.18) | collective-permute-done | bytes 247840 | tf_op jit(solution)/shard_map/ppermute | solution.py:25
  248.4 9.3 %collective-permute-done.19 = f32[2,176,352]{2,1,0:T(8,128)S(1)} collective-permute-done((f32[2,176,352]{2,1,0:T(8,128)S(1)}, f32[2,176,352]{2,1,0:T(8,128)S(1)}, u32[]{:S(2)}, u32[]{:S(2)}) %collective-permute-start.19) | collective-permute-done | bytes 495648 | tf_op jit(solution)/shard_map/ppermute | solution.py:25
  258.7 8.6 %collective-permute-start.20 = (f32[2,176,704]{2,1,0:T(8,128)S(1)}, f32[2,176,704]{2,1,0:T(8,128)}, u32[]{:S(2)}, u32[]{:S(2)}) collective-permute-start(f32[2,176,704]{2,1,0:T(8,128)S(1)} %copy.26), channel_id=1, source_target_pairs={{0,64},{8,72},{16,80},{24,88},{32,96},{40,104},{48,112},{56,120},{... | collective-permute-start | bytes 2973704 | tf_op jit(solution)/shard_map/ppermute | solution.py:25
  267.2 44.9 %collective-permute-done.20 = f32[2,176,704]{2,1,0:T(8,128)} collective-permute-done((f32[2,176,704]{2,1,0:T(8,128)S(1)}, f32[2,176,704]{2,1,0:T(8,128)}, u32[]{:S(2)}, u32[]{:S(2)}) %collective-permute-start.20) | collective-permute-done | bytes 991264 | tf_op jit(solution)/shard_map/ppermute | solution.py:25
  318.0 12.4 %collective-permute-start.29 = (f32[176,176]{1,0:T(8,128)S(1)}, f32[176,176]{1,0:T(8,128)S(1)}, u32[]{:S(2)}, u32[]{:S(2)}) collective-permute-start(f32[176,176]{1,0:T(8,128)S(1)} %copy-done.3), channel_id=1, source_target_pairs={{0,7},{1,0},{2,1},{3,2},{4,3},{5,4},{6,5},{7,6},{8,15},{9,8},{10,9... | collective-permute-start | bytes 371720 | tf_op jit(solution)/shard_map/ppermute | solution.py:17
  347.0 17.9 %reduce-scatter.7.cloned.1.call-done = f32[176,88]{1,0:T(8,128)} async-done(((f32[1408,88]{1,0:T(8,128)}), f32[176,88]{1,0:T(8,128)}) %reduce-scatter.7.cloned.1.call-update) | async-done | bytes 61968 | tf_op jit(solution)/shard_map/reduce_scatter | solution.py:60
  398.3 14.5 %collective-permute-done.24 = f32[176,704]{1,0:T(8,128)S(1)} collective-permute-done((f32[176,704]{1,0:T(8,128)S(1)}, f32[176,704]{1,0:T(8,128)S(1)}, u32[]{:S(2)}, u32[]{:S(2)}) %collective-permute-start.24) | collective-permute-done | bytes 495648 | tf_op jit(solution)/shard_map/ppermute | solution.py:25
  417.6 7.0 %collective-permute-done.32 = f32[2,176,176]{2,1,0:T(8,128)S(1)} collective-permute-done((f32[2,176,176]{2,1,0:T(8,128)S(1)}, f32[2,176,176]{2,1,0:T(8,128)S(1)}, u32[]{:S(2)}, u32[]{:S(2)}) %collective-permute-start.32) | collective-permute-done | bytes 247840 | tf_op jit(solution)/shard_map/ppermute | solution.py:25
  428.3 11.3 %collective-permute-done.33 = f32[2,176,352]{2,1,0:T(8,128)S(1)} collective-permute-done((f32[2,176,352]{2,1,0:T(8,128)S(1)}, f32[2,176,352]{2,1,0:T(8,128)S(1)}, u32[]{:S(2)}, u32[]{:S(2)}) %collective-permute-start.33) | collective-permute-done | bytes 495648 | tf_op jit(solution)/shard_map/ppermute | solution.py:25
  442.6 21.4 %collective-permute-done.34 = f32[2,176,704]{2,1,0:T(8,128)S(1)} collective-permute-done((f32[2,176,704]{2,1,0:T(8,128)S(1)}, f32[2,176,704]{2,1,0:T(8,128)S(1)}, u32[]{:S(2)}, u32[]{:S(2)}) %collective-permute-start.34) | collective-permute-done | bytes 991264 | tf_op jit(solution)/shard_map/ppermute | solution.py:25
  471.0 12.7 %collective-permute-done.38 = f32[176,352]{1,0:T(8,128)S(1)} collective-permute-done((f32[176,352]{1,0:T(8,128)S(1)}, f32[176,352]{1,0:T(8,128)S(1)}, u32[]{:S(2)}, u32[]{:S(2)}) %collective-permute-start.38) | collective-permute-done | bytes 247840 | tf_op jit(solution)/shard_map/ppermute | solution.py:15
  510.5 12.3 %reduce-scatter.9.cloned.1.call-done = f32[176,176]{1,0:T(8,128)} async-done(((f32[1408,176]{1,0:T(8,128)}), f32[176,176]{1,0:T(8,128)}) %reduce-scatter.9.cloned.1.call-update) | async-done | bytes 123920 | tf_op jit(solution)/shard_map/reduce_scatter | solution.py:60
  560.6 9.0 %collective-permute-done.45 = f32[2,176,352]{2,1,0:T(8,128)S(1)} collective-permute-done((f32[2,176,352]{2,1,0:T(8,128)S(1)}, f32[2,176,352]{2,1,0:T(8,128)S(1)}, u32[]{:S(2)}, u32[]{:S(2)}) %collective-permute-start.45) | collective-permute-done | bytes 495648 | tf_op jit(solution)/shard_map/ppermute | solution.py:25
  572.5 20.5 %collective-permute-done.46 = f32[2,176,704]{2,1,0:T(8,128)S(1)} collective-permute-done((f32[2,176,704]{2,1,0:T(8,128)S(1)}, f32[2,176,704]{2,1,0:T(8,128)S(1)}, u32[]{:S(2)}, u32[]{:S(2)}) %collective-permute-start.46) | collective-permute-done | bytes 991264 | tf_op jit(solution)/shard_map/ppermute | solution.py:25
  602.6 51.1 %reduce-scatter.11.cloned.1.call-done = f32[176,352]{1,0:T(8,128)} async-done(((f32[1408,352]{1,0:T(8,128)}), f32[176,352]{1,0:T(8,128)}) %reduce-scatter.11.cloned.1.call-update) | async-done | bytes 247824 | tf_op jit(solution)/shard_map/reduce_scatter | solution.py:60
  (209 shorter events, 234.4 us)
Async XLA Ops:
  7.2 135.8 %reduce-scatter.13.cloned.1.call-start = ((), (), s32[]{:S(2)}) async-start(), calls=%async_computation.7 | async-start | bytes 811008 | tf_op jit(solution)/shard_map/reduce_scatter | solution.py:60
  35.4 11.3 %collective-permute-start.3 = (f32[176,352]{1,0:T(8,128)S(1)}, f32[176,352]{1,0:T(8,128)S(1)}, u32[]{:S(2)}, u32[]{:S(2)}) collective-permute-start(f32[176,352]{1,0:T(8,128)S(1)} %maximum_select_fusion.21), channel_id=1, source_target_pairs={{0,64},{8,72},{16,80},{24,88},{32,96},{40,104},{48,112},{56,120},{... | collective-permute-start | bytes 743432 | tf_op jit(solution)/shard_map/ppermute | solution.py:25
  46.9 52.1 %collective-permute-start.4 = (f32[176,704]{1,0:T(8,128)S(1)}, f32[176,704]{1,0:T(8,128)S(1)}, u32[]{:S(2)}, u32[]{:S(2)}) collective-permute-start(f32[176,704]{1,0:T(8,128)S(1)} %maximum_select_fusion.15), channel_id=1, source_target_pairs={{0,128},{8,136},{16,144},{24,152},{32,160},{40,168},{48,176},{56,1... | collective-permute-start | bytes 1486856 | tf_op jit(solution)/shard_map/ppermute | solution.py:25
  64.4 38.4 %collective-permute-start.15 = (f32[176,88]{1,0:T(8,128)S(1)}, f32[176,88]{1,0:T(8,128)S(1)}, u32[]{:S(2)}, u32[]{:S(2)}) collective-permute-start(f32[176,88]{1,0:T(8,128)S(1)} %collective-permute-done.14), channel_id=1, source_target_pairs={{0,7},{1,0},{2,1},{3,2},{4,3},{5,4},{6,5},{7,6},{8,15},{9,8},{10,9... | collective-permute-start | bytes 185864 | tf_op jit(solution)/shard_map/ppermute | solution.py:17
  69.6 35.7 %collective-permute-start.13 = (f32[176,88]{1,0:T(8,128)S(1)}, f32[176,88]{1,0:T(8,128)S(1)}, u32[]{:S(2)}, u32[]{:S(2)}) collective-permute-start(f32[176,88]{1,0:T(8,128)S(1)} %collective-permute-done.12), channel_id=1, source_target_pairs={{0,1},{1,2},{2,3},{3,4},{4,5},{5,6},{6,7},{7,0},{8,9},{9,10},{10,1... | collective-permute-start | bytes 185864 | tf_op jit(solution)/shard_map/ppermute | solution.py:15
  102.7 262.3 %reduce-scatter.7.cloned.1.call-start = ((), (), s32[]{:S(2)}) async-start(), calls=%async_computation.4 | async-start | bytes 811008 | tf_op jit(solution)/shard_map/reduce_scatter | solution.py:60
  102.9 59.4 %collective-permute-start.16 = (f32[176,88]{1,0:T(8,128)S(1)}, f32[176,88]{1,0:T(8,128)S(1)}, u32[]{:S(2)}, u32[]{:S(2)}) collective-permute-start(f32[176,88]{1,0:T(8,128)S(1)} %collective-permute-done.15), channel_id=1, source_target_pairs={{0,7},{1,0},{2,1},{3,2},{4,3},{5,4},{6,5},{7,6},{8,15},{9,8},{10,9... | collective-permute-start | bytes 185864 | tf_op jit(solution)/shard_map/ppermute | solution.py:17
  167.9 12.1 %collective-permute-start.8 = (f32[176,352]{1,0:T(8,128)S(1)}, f32[176,352]{1,0:T(8,128)S(1)}, u32[]{:S(2)}, u32[]{:S(2)}) collective-permute-start(f32[176,352]{1,0:T(8,128)S(1)} %maximum_select_fusion.22), channel_id=1, source_target_pairs={{0,64},{8,72},{16,80},{24,88},{32,96},{40,104},{48,112},{56,120},{... | collective-permute-start | bytes 743432 | tf_op jit(solution)/shard_map/ppermute | solution.py:25
  180.2 46.0 %collective-permute-start.9 = (f32[176,704]{1,0:T(8,128)S(1)}, f32[176,704]{1,0:T(8,128)S(1)}, u32[]{:S(2)}, u32[]{:S(2)}) collective-permute-start(f32[176,704]{1,0:T(8,128)S(1)} %maximum_select_fusion.16), channel_id=1, source_target_pairs={{0,128},{8,136},{16,144},{24,152},{32,160},{40,168},{48,176},{56,1... | collective-permute-start | bytes 1486856 | tf_op jit(solution)/shard_map/ppermute | solution.py:25
  258.7 53.5 %collective-permute-start.20 = (f32[2,176,704]{2,1,0:T(8,128)S(1)}, f32[2,176,704]{2,1,0:T(8,128)}, u32[]{:S(2)}, u32[]{:S(2)}) collective-permute-start(f32[2,176,704]{2,1,0:T(8,128)S(1)} %copy.26), channel_id=1, source_target_pairs={{0,64},{8,72},{16,80},{24,88},{32,96},{40,104},{48,112},{56,120},{... | collective-permute-start | bytes 2973704 | tf_op jit(solution)/shard_map/ppermute | solution.py:25
  267.2 50.7 %collective-permute-start.25 = (f32[176,176]{1,0:T(8,128)S(1)}, f32[176,176]{1,0:T(8,128)S(1)}, u32[]{:S(2)}, u32[]{:S(2)}) collective-permute-start(f32[176,176]{1,0:T(8,128)S(1)} %copy-done.3), channel_id=1, source_target_pairs={{0,1},{1,2},{2,3},{3,4},{4,5},{5,6},{6,7},{7,0},{8,9},{9,10},{10,1... | collective-permute-start | bytes 371720 | tf_op jit(solution)/shard_map/ppermute | solution.py:15
  317.7 205.1 %reduce-scatter.9.cloned.1.call-start = ((), (), s32[]{:S(2)}) async-start(), calls=%async_computation.5 | async-start | bytes 1622016 | tf_op jit(solution)/shard_map/reduce_scatter | solution.py:60
  317.9 15.6 %collective-permute-start.26 = (f32[176,176]{1,0:T(8,128)S(1)}, f32[176,176]{1,0:T(8,128)S(1)}, u32[]{:S(2)}, u32[]{:S(2)}) collective-permute-start(f32[176,176]{1,0:T(8,128)S(1)} %collective-permute-done.25), channel_id=1, source_target_pairs={{0,1},{1,2},{2,3},{3,4},{4,5},{5,6},{6,7},{7,0},{8,9},{9,10},{10,1... | collective-permute-start | bytes 371720 | tf_op jit(solution)/shard_map/ppermute | solution.py:15
  318.0 15.6 %collective-permute-start.29 = (f32[176,176]{1,0:T(8,128)S(1)}, f32[176,176]{1,0:T(8,128)S(1)}, u32[]{:S(2)}, u32[]{:S(2)}) collective-permute-start(f32[176,176]{1,0:T(8,128)S(1)} %copy-done.3), channel_id=1, source_target_pairs={{0,7},{1,0},{2,1},{3,2},{4,3},{5,4},{6,5},{7,6},{8,15},{9,8},{10,9... | collective-permute-start | bytes 371720 | tf_op jit(solution)/shard_map/ppermute | solution.py:17
  339.7 37.9 %collective-permute-start.31 = (f32[176,176]{1,0:T(8,128)}, f32[176,176]{1,0:T(8,128)}, u32[]{:S(2)}, u32[]{:S(2)}) collective-permute-start(f32[176,176]{1,0:T(8,128)} %collective-permute-done.30), channel_id=1, source_target_pairs={{0,7},{1,0},{2,1},{3,2},{4,3},{5,4},{6,5},{7,6},{8,15},{9,8},{10,9... | collective-permute-start | bytes 371720 | tf_op jit(solution)/shard_map/ppermute | solution.py:17
  392.1 20.8 %collective-permute-start.24 = (f32[176,704]{1,0:T(8,128)S(1)}, f32[176,704]{1,0:T(8,128)S(1)}, u32[]{:S(2)}, u32[]{:S(2)}) collective-permute-start(f32[176,704]{1,0:T(8,128)S(1)} %maximum_select_fusion.17), channel_id=1, source_target_pairs={{0,64},{8,72},{16,80},{24,88},{32,96},{40,104},{48,112},{56,120},{... | collective-permute-start | bytes 1486856 | tf_op jit(solution)/shard_map/ppermute | solution.py:25
  424.8 14.8 %collective-permute-start.33 = (f32[2,176,352]{2,1,0:T(8,128)S(1)}, f32[2,176,352]{2,1,0:T(8,128)S(1)}, u32[]{:S(2)}, u32[]{:S(2)}) collective-permute-start(f32[2,176,352]{2,1,0:T(8,128)S(1)} %maximum_select_fusion.18), channel_id=1, source_target_pairs={{0,16},{8,24},{16,0},{24,8},{32,48},{40,56},{48,32},{56,40},{64,80... | collective-permute-start | bytes 1486856 | tf_op jit(solution)/shard_map/ppermute | solution.py:25
  440.1 23.9 %collective-permute-start.34 = (f32[2,176,704]{2,1,0:T(8,128)S(1)}, f32[2,176,704]{2,1,0:T(8,128)S(1)}, u32[]{:S(2)}, u32[]{:S(2)}) collective-permute-start(f32[2,176,704]{2,1,0:T(8,128)S(1)} %maximum_select_fusion.4), channel_id=1, source_target_pairs={{0,32},{8,40},{16,48},{24,56},{32,0},{40,8},{48,16},{56,24},{64,96... | collective-permute-start | bytes 2973704 | tf_op jit(solution)/shard_map/ppermute | solution.py:25
  470.9 182.7 %reduce-scatter.11.cloned.1.call-start = ((), (), s32[]{:S(2)}) async-start(), calls=%async_computation.6 | async-start | bytes 2433024 | tf_op jit(solution)/shard_map/reduce_scatter | solution.py:60
  470.9 12.7 %collective-permute-start.38 = (f32[176,352]{1,0:T(8,128)S(1)}, f32[176,352]{1,0:T(8,128)S(1)}, u32[]{:S(2)}, u32[]{:S(2)}) collective-permute-start(f32[176,352]{1,0:T(8,128)S(1)} %copy-done), channel_id=1, source_target_pairs={{0,1},{1,2},{2,3},{3,4},{4,5},{5,6},{6,7},{7,0},{8,9},{9,10},{10,1... | collective-permute-start | bytes 743432 | tf_op jit(solution)/shard_map/ppermute | solution.py:15
  497.9 28.0 %collective-permute-start.44 = (f32[176,352]{1,0:T(8,128)S(1)}, f32[176,352]{1,0:T(8,128)S(1)}, u32[]{:S(2)}, u32[]{:S(2)}) collective-permute-start(f32[176,352]{1,0:T(8,128)S(1)} %collective-permute-done.43), channel_id=1, source_target_pairs={{0,7},{1,0},{2,1},{3,2},{4,3},{5,4},{6,5},{7,6},{8,15},{9,8},{10,9... | collective-permute-start | bytes 743432 | tf_op jit(solution)/shard_map/ppermute | solution.py:17
  541.7 11.3 %collective-permute-start.37 = (f32[176,704]{1,0:T(8,128)S(1)}, f32[176,704]{1,0:T(8,128)S(1)}, u32[]{:S(2)}, u32[]{:S(2)}) collective-permute-start(f32[176,704]{1,0:T(8,128)S(1)} %maximum_select_fusion.19), channel_id=1, source_target_pairs={{0,32},{8,40},{16,48},{24,56},{32,0},{40,8},{48,16},{56,24},{64,96... | collective-permute-start | bytes 1486856 | tf_op jit(solution)/shard_map/ppermute | solution.py:25
  556.9 12.7 %collective-permute-start.45 = (f32[2,176,352]{2,1,0:T(8,128)S(1)}, f32[2,176,352]{2,1,0:T(8,128)S(1)}, u32[]{:S(2)}, u32[]{:S(2)}) collective-permute-start(f32[2,176,352]{2,1,0:T(8,128)S(1)} %pad_maximum_fusion), channel_id=1, source_target_pairs={{0,8},{8,0},{16,24},{24,16},{32,40},{40,32},{48,56},{56,48},{64,72... | collective-permute-start | bytes 1486856 | tf_op jit(solution)/shard_map/ppermute | solution.py:25
  570.1 23.0 %collective-permute-start.46 = (f32[2,176,704]{2,1,0:T(8,128)S(1)}, f32[2,176,704]{2,1,0:T(8,128)S(1)}, u32[]{:S(2)}, u32[]{:S(2)}) collective-permute-start(f32[2,176,704]{2,1,0:T(8,128)S(1)} %maximum_select_fusion.5), channel_id=1, source_target_pairs={{0,16},{8,24},{16,0},{24,8},{32,48},{40,56},{48,32},{56,40},{64,80... | collective-permute-start | bytes 2973704 | tf_op jit(solution)/shard_map/ppermute | solution.py:25
  (45 other events, 627.2 us)
Sparse Core Ops, SparseCore 0:
  102.8 40.1 reduce-scatter.12
  317.8 47.0 reduce-scatter.6
  471.0 51.7 reduce-scatter.8
  600.4 53.1 reduce-scatter.10
